TPU v7x, 32 devices: a whole 2x2x4 slice. The times are simulated.
32 devices in a mesh: dp: 4 (over x, core), fsdp: 2 (over y), ctx: 4 (over z).
Axes of the slice: x: 2, y: 2, z: 4, core: 2. Of those that a mesh axis runs over, the one named last changes fastest.
Arguments:
- box_hidden_states: bfloat16 [8, 2048, 8192], P(('dp', 'fsdp'), 'ctx'), may hold values from -60 to 60
- box_token_positions: int32 [8, 2048], P(('dp', 'fsdp')), may hold values from 0 to 8191, as said below
- document_lengths: int32 [8, 3], P(('dp', 'fsdp')), may hold values from 512 to 7168, as said below
- successors: int32 [8, 2048], P(('dp', 'fsdp'), 'ctx'), may hold values from 0 to 2047, as said below
- fixed_key_matrix: bfloat16 [8192, 1024], P('fsdp'), may hold values from -0.0625 to 0.0625
- adapter_down: bfloat16 [8192, 16], replicated, may hold values from -0.0625 to 0.0625
- adapter_up: bfloat16 [16, 1024], replicated, may hold values from -1.5 to 1.5
- pointer_query_map: bfloat16 [1024, 64], replicated, may hold values from -0.1875 to 0.1875
- pointer_key_map: bfloat16 [1024, 64], replicated, may hold values from -0.1875 to 0.1875
Outputs:
- grad_down: float32 [8192, 16], P('fsdp')
- up_gradient: float32 [16, 1024], replicated
- grad_query: float32 [1024, 64], replicated
- grad_key: float32 [1024, 64], replicated
- mean_loss: float32 [], replicated
Inputs may be any that keep to these rules, and one draw needn't show every extreme that they name: `box_token_positions`: each row is increasing; entries k * 512 to (k + 1) * 512 - 1 lie in positions k * 2048 to (k + 1) * 2048 - 1. `document_lengths`: each row holds multiples of 512 that sum to 8192. `successors`: the index of a box token of the same sequence and the same document as the query; the query itself only where it is the document's only box token or so drawn.
All inputs are finite; a program needn't handle non-finite values.
Results may differ from a plain program's by a relative error of at most 0.012.
The roundings to bfloat16 on the way count: a program that leaves them out, or rounds other values in their place, can miss the bound.
Values may be sent and summed in bfloat16 or wider, within the bound.
A program may use at most 128 MiB of HBM per device.

v0:
```python
import math

import jax
import jax.numpy as jnp
from jax import lax
from jax.sharding import PartitionSpec as P

ADAPTER_SCALE = 0.5


def contract_rows(left, right):
    return lax.dot_general(
        left, right, (((0,), (0,)), ((), ())), preferred_element_type=jnp.float32
    )


def contracted_columns(left, right):
    return lax.dot_general(
        left, right, (((1,), (1,)), ((), ())), preferred_element_type=jnp.float32
    )


def precise_rows(left, right):
    return lax.dot_general(
        left.astype(jnp.float32),
        right,
        (((0,), (0,)), ((), ())),
        precision=lax.Precision.HIGHEST,
        preferred_element_type=jnp.float32,
    )


def precise_columns(left, right):
    return lax.dot_general(
        left,
        right.astype(jnp.float32),
        (((1,), (1,)), ((), ())),
        precision=lax.Precision.HIGHEST,
        preferred_element_type=jnp.float32,
    )


def on_device(
    box_hidden_states,
    box_token_positions,
    document_lengths,
    successors,
    fixed_key_matrix,
    adapter_down,
    adapter_up,
    pointer_query_map,
    pointer_key_map,
):
    hidden_states = box_hidden_states[0]
    count = hidden_states.shape[0]
    groups = lax.axis_size("fsdp")
    seqs_all = lax.axis_size("dp") * groups
    ctx_count = lax.axis_size("ctx")
    width = pointer_query_map.shape[1]
    scale = 1.0 / math.sqrt(width)
    pointer_heads = jnp.concatenate([pointer_query_map, pointer_key_map], axis=1)
    adapter_pointer = jnp.dot(adapter_up, pointer_heads, preferred_element_type=jnp.float32).astype(
        jnp.bfloat16
    )
    complete_keys = lax.all_gather(fixed_key_matrix, "fsdp", axis=0, tiled=True)
    pointer_logits = jnp.dot(
        complete_keys, pointer_heads, preferred_element_type=jnp.float32
    ).astype(jnp.bfloat16)
    projected_states = jnp.dot(hidden_states, pointer_logits, preferred_element_type=jnp.float32)
    narrow_rows = jnp.dot(hidden_states, adapter_down, preferred_element_type=jnp.float32).astype(
        jnp.bfloat16
    )
    blended_terms = (
        projected_states
        + ADAPTER_SCALE * jnp.dot(narrow_rows, adapter_pointer, preferred_element_type=jnp.float32)
    ).astype(jnp.bfloat16)
    queries = blended_terms[:, :width]
    keys = blended_terms[:, width:]
    all_keys = lax.all_gather(keys, "ctx", axis=0, tiled=True)
    ends = jnp.cumsum(document_lengths[0])
    segment = jnp.sum(
        (box_token_positions[0][:, None] >= ends[None, :-1]).astype(jnp.int32), axis=1
    )
    own_segment = lax.dynamic_slice_in_dim(segment, lax.axis_index("ctx") * count, count)
    scores = contracted_columns(queries, all_keys) * scale
    same = own_segment[:, None] == segment[None, :]
    masked = jnp.where(same, scores, -jnp.inf)
    top = jnp.max(masked, axis=1, keepdims=True)
    total = jnp.sum(jnp.exp(masked - top), axis=1, keepdims=True)
    lse = top + jnp.log(total)
    column = jnp.arange(scores.shape[1], dtype=jnp.int32)
    hit = column[None, :] == successors[0][:, None]
    picked = jnp.sum(jnp.where(hit, scores, 0.0), axis=1)
    loss_part = jnp.sum(lse[:, 0] - picked)
    prob = jnp.exp(masked - lse)
    weights = ((prob - hit.astype(jnp.float32)) * (scale * (1.0 / seqs_all))).astype(jnp.bfloat16)
    grad_q = jnp.dot(weights, all_keys, preferred_element_type=jnp.float32).astype(jnp.bfloat16)
    grad_k = lax.psum_scatter(
        contract_rows(weights, queries), "ctx", scatter_dimension=0, tiled=True
    ).astype(jnp.bfloat16)
    paired_terms = jnp.concatenate([grad_q, grad_k], axis=1)
    narrow_gradient = (ADAPTER_SCALE * contracted_columns(paired_terms, adapter_pointer)).astype(
        jnp.bfloat16
    )
    projection_gradient = contract_rows(hidden_states, paired_terms)
    narrow_rows_gradient = contract_rows(narrow_rows, paired_terms)
    grad_down = contract_rows(hidden_states, narrow_gradient)
    denominator = seqs_all * count * ctx_count
    rows_each = grad_down.shape[0] // groups
    summed_terms = lax.psum(
        (grad_down, projection_gradient, narrow_rows_gradient, loss_part), ("dp", "fsdp", "ctx")
    )
    head_gradients = precise_rows(complete_keys, summed_terms[1]) + ADAPTER_SCALE * precise_rows(
        adapter_up, summed_terms[2]
    )
    up_gradient = ADAPTER_SCALE * precise_columns(summed_terms[2], pointer_heads)
    down_rows = lax.dynamic_slice_in_dim(
        summed_terms[0], lax.axis_index("fsdp") * rows_each, rows_each, 0
    )
    return (
        down_rows,
        up_gradient,
        head_gradients[:, :width],
        head_gradients[:, width:],
        summed_terms[3] / denominator,
    )


def solution(mesh):
    in_specs = (
        P(("dp", "fsdp"), "ctx", None),
        P(("dp", "fsdp"), None),
        P(("dp", "fsdp"), None),
        P(("dp", "fsdp"), "ctx"),
        P("fsdp", None),
        P(),
        P(),
        P(),
        P(),
    )
    out_specs = (P("fsdp", None), P(), P(), P(), P())
    return jax.shard_map(
        on_device, mesh=mesh, in_specs=in_specs, out_specs=out_specs, check_vma=False
    )
```

profile of v0, /device:TPU:0, one launch (start us, length us, event | category | flops | bytes accessed | tf_op | source)
XLA Modules:
  0.0 445.7 jit_solution(16629726569500244938)
XLA Ops:
  7.2 0.0 all-gather.2.cloned.1.call-start
  7.3 0.7 all-gather.2.cloned.1.call-update
  8.0 0.0 reduce-scatter.2.cloned.1.call-start
  8.0 0.2 reduce-window.4
  8.2 0.1 fusion.24
  8.3 0.1 dynamic_slice.6
  8.4 0.2 convolution_convert_fusion.2
  8.6 5.7 %fusion.15 = bf16[512,16]{0,1:T(8,128)(2,1)S(1)} fusion(bf16[8192,16]{0,1:T(8,128)(2,1)S(1)} %copy-done, bf16[1,512,8192]{2,1,0:T(8,128)(2,1)} %param.9), kind=kOutput, calls=%fused_computation.26 | convolution fusion | flops 134225920 | bytes 8667136 | tf_op jit(solution)/shard_map/dot_general | solution.py:70
  14.3 196.9 %all-gather.2.cloned.1.call-done = bf16[8192,1024]{1,0:T(8,128)(2,1)} async-done(((bf16[4096,1024]{1,0:T(8,128)(2,1)}), bf16[8192,1024]{1,0:T(8,128)(2,1)}) %all-gather.2.cloned.1.call-update) | async-done | bytes 16777232 | tf_op jit(solution)/shard_map/all_gather | solution.py:65
  211.2 13.1 %fusion.10 = f32[512,128]{0,1:T(8,128)S(1)} fusion(bf16[1,512,8192]{2,1,0:T(8,128)(2,1)} %param.9, bf16[1024,128]{0,1:T(8,128)(2,1)S(1)} %constant_dynamic-update-slice_fusion, bf16[8192,1024]{1,0:T(8,128)(2,1)} %all-gather.2.cloned.1.call-done), kind=kOutput, calls=%fused_computation.21 | convolution fusion | flops 3222274048 | bytes 25690112 | tf_op jit(solution)/shard_map/dot_general | solution.py:69
  224.4 0.2 fusion.13
  224.6 13.9 %all_gather.7 = bf16[2048,64]{0,1:T(8,128)(2,1)S(1)} all-gather(bf16[512,64]{0,1:T(8,128)(2,1)S(1)} %slice.22), channel_id=1, replica_groups=mesh['dp'=4,'fsdp'=2,'ctx'=4] {'ctx'}, dimensions={0}, use_global_device_ids=true | all-gather | bytes 327680 | tf_op jit(solution)/shard_map/all_gather | solution.py:79
  238.6 0.9 fusion.6
  239.4 2.1 select_reduce_fusion
  241.5 0.6 subtract_reduce_fusion
  242.1 1.9 multiply_convert_fusion
  244.0 1.3 fusion.19
  245.3 0.0 reduce-scatter.2.cloned.1.call-update
  245.3 0.2 all-reduce.4.cloned.1.call-start
  245.5 0.8 convolution_convert_fusion.1
  246.3 21.2 %reduce-scatter.2.cloned.1.call-done = f32[512,64]{0,1:T(8,128)} async-done(((f32[2048,64]{0,1:T(8,128)}), f32[512,64]{0,1:T(8,128)}) %reduce-scatter.2.cloned.1.call-update) | async-done | bytes 131088 | tf_op jit(solution)/shard_map/reduce_scatter | solution.py:98
  267.5 0.9 convert_element_type.43
  268.4 5.7 %convolution_bitcast_fusion.1 = f32[8192,16]{0,1:T(8,128)} fusion(bf16[1,512,8192]{2,1,0:T(8,128)(2,1)} %param.9, bf16[128,16]{0,1:T(8,128)(2,1)S(1)} %convolution_convert_fusion.2, bf16[512,64]{0,1:T(8,128)(2,1)S(1)} %convert_element_type.43, bf16[512,64]{0,1:T(8,128)(2,1)S(1)} %convolution_convert_fusion.1), kind=kOutput, calls=%fused_computation.2 | convolution fusion | flops 136593408 | bytes 9048064 | tf_op jit(solution)/shard_map/dot_general | solution.py:12
  274.1 6.6 %convolution_bitcast_fusion = f32[8192,128]{0,1:T(8,128)} fusion(bf16[1,512,8192]{2,1,0:T(8,128)(2,1)} %param.9, bf16[512,64]{0,1:T(8,128)(2,1)S(1)} %convert_element_type.43, bf16[512,64]{0,1:T(8,128)(2,1)S(1)} %convolution_convert_fusion.1), kind=kOutput, calls=%fused_computation | convolution fusion | flops 1074003968 | bytes 12713984 | tf_op jit(solution)/shard_map/dot_general | solution.py:12
  280.8 0.1 fusion.23
  280.9 39.2 %all-reduce = (f32[16,128]{1,0:T(8,128)S(1)}, f32[]{:T(128)}) all-reduce(f32[16,128]{1,0:T(8,128)S(1)} %fusion.23, f32[]{:T(128)} %get-tuple-element.11), channel_id=1, replica_groups=mesh['dp'=4,'fsdp'=2,'ctx'=4] {'dp','fsdp','ctx'}, use_global_device_ids=true, to_apply=%region_6.7 | all-reduce | flops 2049 | bytes 16392 | tf_op jit(solution)/shard_map/psum | solution.py:110
  320.7 0.9 convolution_multiply_fusion.3
  321.6 102.4 %all-reduce.4.cloned.1.call-done = (f32[8192,16]{0,1:T(8,128)}, f32[8192,128]{0,1:T(8,128)}) async-done(((f32[8192,16]{0,1:T(8,128)}, f32[8192,128]{0,1:T(8,128)}), (f32[8192,16]{0,1:T(8,128)}, f32[8192,128]{0,1:T(8,128)})) %all-reduce.4.cloned.1.call-update) | async-done | bytes 4718608 | tf_op jit(solution)/shard_map/psum | solution.py:110
  424.0 12.0 %fusion.31 = f32[128,1024]{1,0:T(8,128)S(1)} fusion(f32[8192,128]{0,1:T(8,128)} %get-tuple-element.10, bf16[8192,1024]{1,0:T(8,128)(2,1)} %all-gather.2.cloned.1.call-done), kind=kOutput, calls=%fused_computation.48 | convolution fusion | flops 12884901888 | bytes 21495808 | tf_op jit(solution)/shard_map/dot_general | solution.py:24
  436.1 0.4 fusion.8
  436.5 0.8 fusion.30
  437.3 0.7 constant_dynamic-slice_fusion
  (21 shorter events, 0.1 us)
Async XLA Ops:
  7.2 1.5 copy-start
  7.2 0.8 copy-start.7
  7.2 1.0 copy-start.6
  7.2 1.2 copy-start.3
  7.2 1.2 copy-start.4
  7.2 1.2 copy-start.1
  7.2 204.0 %all-gather.2.cloned.1.call-start = ((), (), s32[]{:S(2)}) async-start(), calls=%async_computation.1 | async-start | bytes 25165824 | tf_op jit(solution)/shard_map/all_gather | solution.py:65
  8.0 259.6 %reduce-scatter.2.cloned.1.call-start = ((), (), s32[]{:S(2)}) async-start(), calls=%async_computation.2 | async-start | bytes 655360 | tf_op jit(solution)/shard_map/reduce_scatter | solution.py:98
  224.4 15.1 %copy-start.5 = (s32[1,512]{1,0:T(1,128)S(1)}, s32[1,512]{1,0:T(1,128)}, u32[]{:S(2)}) copy-start(s32[1,512]{1,0:T(1,128)} %param.12) | copy-start | bytes 6148
  245.3 178.7 %all-reduce.4.cloned.1.call-start = ((), (), s32[]{:S(2)}) async-start(), calls=%async_computation.3 | async-start | bytes 9437184 | tf_op jit(solution)/shard_map/psum | solution.py:110
  424.0 13.3 %copy-start.2 = (f32[8192,16]{0,1:T(8,128)S(1)}, f32[8192,16]{0,1:T(8,128)}, u32[]{:S(2)}) copy-start(f32[8192,16]{0,1:T(8,128)} %get-tuple-element.9) | copy-start | bytes 1572868
Sparse Core Ops, SparseCore 0:
  9.6 201.5 all-gather.1
  245.4 22.0 reduce-scatter.1
  280.9 143.0 all-reduce.3
where the time goes:
time: 446 us
  waiting for transfers between devices  321 us (72%)
  blocking collectives  53.1 us (12%)
  matrix products  47.9 us (11%)
  between operations  15.7 us (4%)
  other arithmetic  5.73 us (1%)
    all_gather x1, waiting for transfers between devices, on_device(): complete_keys = lax.all_gather(fixed_key_matrix, 'fsdp', axis=0, tiled=True)  197 us
    psum x1, waiting for transfers between devices, on_device(): lax.psum((grad_down, projection_gradient, narrow_rows_gradient, loss_part...  102 us
    psum x1, blocking collectives, on_device(): lax.psum((grad_down, projection_gradient, narrow_rows_gradient, loss_part...  39.2 us
    reduce_scatter x1, waiting for transfers between devices, on_device(): lax.psum_scatter(contract_rows(weights, queries), 'ctx', scatter_dimensio...  21.2 us
    all_gather x1, blocking collectives, on_device(): all_keys = lax.all_gather(keys, 'ctx', axis=0, tiled=True)  13.9 us
    dot_general x4, matrix products, contract_rows(): lax.dot_general(left, right, (((0,), (0,)), ((), ())), preferred_element_...  13.7 us
    dot_general x1, matrix products, on_device(): jnp.dot(hidden_states, pointer_logits, preferred_element_type=jnp.float32)  13.1 us
    dot_general x2, matrix products, precise_rows(): lax.dot_general(left.astype(jnp.float32), right, (((0,), (0,)), ((), ()))...  12.5 us
  transfers between devices with their start and end apart: 3, of which 3 were waited for; matrix products, arithmetic and copies ran while one was open for 2% of the time, Pallas kernels for 0%

commit v1 on v0

v1 whole, which is shorter than its diff:
```python
import functools
import math

import jax
import jax.numpy as jnp
from jax import lax
from jax.experimental import pallas as pl
from jax.experimental.pallas import tpu as pltpu
from jax.sharding import PartitionSpec as P

ADAPTER_SCALE = 0.5
BF = jnp.bfloat16
F32 = jnp.float32


def mm(a, b):
    return lax.dot_general(a, b, (((1,), (0,)), ((), ())), preferred_element_type=F32)


def mm_t(a, b):
    return lax.dot_general(a, b, (((1,), (1,)), ((), ())), preferred_element_type=F32)


def at(start, size, unit):
    return pl.ds(pl.multiple_of(start, unit), size)


def kernel(
    D, F, C, seqs_all,
    h_hbm, k_hbm, down_t, up, heads, pos, lengths, succ,
    o_grad, o_up, o_down, o_loss,
    hbuf, kbuf, pbuf, acc, lowacc, bl, blt, keys_t, wts, seg_col, succ_col,
    gks, gkr, g_t, core_s, core_r, own, y_s, y_r, proj,
    pay, r1, p2, r2, p3, r3, fin, gd, gd_x, gd2, gd_r, gd_all,
    load_sem, send_sem, recv_sem,
):
    rows_all, rank = hbuf.shape[1], up.shape[0]
    count, width = hbuf.shape[0], bl.shape[1] // 2
    RF = rows_all // F
    PC = RF // 2
    SUB = PC // 2
    dp, f, ctx = lax.axis_index("dp"), lax.axis_index("fsdp"), lax.axis_index("ctx")
    par = lax.rem(dp, 2)
    mate = dp + 1 - 2 * par
    other = 1 - par

    loads = []

    def load(src, dst):
        cp = pltpu.make_async_copy(src, dst, load_sem.at[len(loads)])
        cp.start()
        loads.append(cp)
        return cp

    def krows(p, s):
        return at(p * PC + s * SUB, SUB, SUB)

    lk = [
        load(k_hbm.at[krows(p, s)], kbuf.at[krows(p, s)])
        for p in (par, other)
        for s in (0, 1)
    ]
    lh = []
    for k in range(F):
        cols = at(lax.rem(f + k, F) * RF, RF, 128)
        lh.append(load(h_hbm.at[:, cols], hbuf.at[:, cols]))

    axes = {"dp": (dp, D), "fsdp": (f, F), "ctx": (ctx, C)}

    def peer(axis, k):
        me, n = axes[axis]
        return lax.rem(me + k, n)

    barrier = pltpu.get_barrier_semaphore()
    for axis in axes:
        for k in range(1, axes[axis][1]):
            pl.semaphore_signal(
                barrier, inc=1, device_id={axis: peer(axis, k)},
                device_id_type=pl.DeviceIdType.MESH,
            )

    sent = []

    def send(src, dst, axis, target):
        i = len(sent)
        cp = pltpu.make_async_remote_copy(
            src_ref=src, dst_ref=dst, send_sem=send_sem.at[i], recv_sem=recv_sem.at[i],
            device_id={axis: target}, device_id_type=pl.DeviceIdType.MESH,
        )
        cp.start()
        sent.append(cp)
        return cp

    hd = heads[...]
    tile = min(512, SUB)

    def pointer_rows(p, s):
        def body(t, _):
            r = p * PC + s * SUB + t * tile
            pbuf[at(f * RF + r, tile, tile), :] = mm(kbuf[at(r, tile, tile), :], hd).astype(BF)
            return 0
        lax.fori_loop(0, SUB // tile, body, 0)

    def grows(g, p, s):
        return at(g * RF + p * PC + s * SUB, SUB, SUB)

    ysend = {}
    for s in (0, 1):
        lk[s].wait()
        pointer_rows(par, s)
        if s == 0:
            pl.semaphore_wait(barrier, (D - 1) + (F - 1) + (C - 1))
        for k in range(1, F):
            r = grows(f, par, s)
            ysend[s, k] = send(pbuf.at[r], pbuf.at[r], "fsdp", peer("fsdp", k))
    for s in (0, 1):
        lk[2 + s].wait()
        pointer_rows(other, s)

    adapter = mm(up[...], hd).astype(BF)

    def add_rows(start, n):
        def body(t, _):
            c = at(start + t * tile, tile, 128)
            acc[...] += mm(hbuf[:, c], pbuf[at(start + t * tile, tile, tile), :])
            return 0
        lax.fori_loop(0, n // tile, body, 0)

    acc[...] = jnp.zeros_like(acc)
    lowacc[...] = jnp.zeros_like(lowacc)
    lh[0].wait()
    add_rows(f * RF, RF)
    for k in range(1, F):
        lh[k].wait()

    def low_body(t, _):
        c = at(t * 1024, 1024, 128)
        lowacc[...] += mm_t(hbuf[:, c], down_t[:, c])
        return 0
    lax.fori_loop(0, rows_all // 1024, low_body, 0)
    low = lowacc[...].astype(BF)
    acc[...] += ADAPTER_SCALE * mm(low, adapter)

    def to_column(row):
        return jnp.broadcast_to(row, (128, count)).T

    def segment_of(p):
        end = jnp.zeros((1, 1), jnp.int32)
        total = jnp.zeros(p.shape, F32)
        for n in range(lengths.shape[1] - 1):
            end = end + lengths[:, n : n + 1]
            total = total + jnp.where(p >= end, 1.0, 0.0)
        return total

    seg_row = segment_of(pos[...])
    seg_col[...] = to_column(segment_of(pos[:, at(ctx * count, count, 128)]))
    succ_col[...] = to_column(succ[...].astype(F32))

    relayed = {}
    for s in (0, 1):
        for k in range(1, F):
            g = peer("fsdp", F - k)
            ysend[s, k].wait_recv()
            r = grows(g, par, s)
            relayed[s, k] = send(pbuf.at[r], pbuf.at[r], "dp", mate)
            add_rows(g * RF + par * PC + s * SUB, SUB)
    for s in (0, 1):
        for k in range(1, F):
            relayed[s, k].wait_recv()
            add_rows(peer("fsdp", F - k) * RF + other * PC + s * SUB, SUB)

    rounded = acc[...].astype(BF)
    bl[...] = rounded
    blt[...] = rounded.astype(F32).T.astype(BF)
    keys_t[ctx] = blt[width:, :]
    kcp = [
        send(keys_t.at[ctx], keys_t.at[ctx], "ctx", peer("ctx", k)) for k in range(1, C)
    ]
    for cp in kcp:
        cp.wait_recv()

    scale = 1.0 / math.sqrt(width)
    block = 64
    column = lax.broadcasted_iota(jnp.int32, (1, C * count), 1).astype(F32)

    def soft(t, loss):
        r = at(t * block, block, block)
        q = bl[r, :width]
        sc = jnp.concatenate([mm(q, keys_t[j]) for j in range(C)], axis=1) * scale
        masked = jnp.where(seg_col[r, 0:1] == seg_row, sc, -jnp.inf)
        top = jnp.max(masked, axis=1, keepdims=True)
        e = jnp.exp(masked - top)
        total = jnp.sum(e, axis=1, keepdims=True)
        hit = succ_col[r, 0:1] == column
        picked = jnp.sum(jnp.where(hit, sc, 0.0), axis=1, keepdims=True)
        ws = scale / seqs_all
        wts[r, :] = (e * (ws / total) - jnp.where(hit, ws, 0.0)).astype(BF)
        return loss + (top + jnp.log(total) - picked)

    loss = lax.fori_loop(0, count // block, soft, jnp.zeros((block, 1), F32))
    loss = jnp.sum(loss, axis=0, keepdims=True)

    q_t = blt[:width, :]
    gcp = []
    for k in range(1, C):
        c = at(peer("ctx", k) * count, count, 128)
        gks[k - 1] = mm(q_t, wts[:, c]).astype(BF)
        gcp.append(send(gks.at[k - 1], gkr.at[k - 1], "ctx", peer("ctx", k)))
    gq = mm_t(keys_t[0], wts[:, :count])
    for j in range(1, C):
        gq = gq + mm_t(keys_t[j], wts[:, j * count : (j + 1) * count])
    g_t[0] = gq.astype(BF)
    gk = mm(q_t, wts[:, at(ctx * count, count, 128)])

    ct = min(512, PC)

    def half_start(h):
        g = g_t[h]
        cps = []
        for k in list(range(1, F)) + [0]:
            base = peer("fsdp", k) * RF
            for t in range(PC // ct):
                core_s[h, k, :, t * ct : (t + 1) * ct] = mm(
                    g, hbuf[:, at(base + other * PC + t * ct, ct, 128)]
                ).astype(BF)
            cps.append((k, send(core_s.at[h, k], core_r.at[h, k], "dp", mate)))
        for k in range(F):
            base = peer("fsdp", k) * RF
            for t in range(PC // ct):
                own[h, k, :, t * ct : (t + 1) * ct] = mm(
                    g, hbuf[:, at(base + par * PC + t * ct, ct, 128)]
                )
        ys = []
        for k, cp in cps:
            cp.wait_recv()
            summed = own[h, k] + core_r[h, k].astype(F32)
            if k:
                y_s[h, k - 1] = summed.astype(BF)
                ys.append(
                    (k, send(y_s.at[h, k - 1], y_r.at[h, k - 1], "fsdp", peer("fsdp", k)))
                )
            else:
                own[h, 0] = summed
        return ys

    def half_end(h, ys):
        total = own[h, 0]
        for k, cp in ys:
            cp.wait_recv()
            total = total + y_r[h, k - 1].astype(F32)
        proj[h * width : (h + 1) * width, :] = total.astype(BF)

    yq = half_start(0)
    for k in range(1, C):
        gcp[k - 1].wait_recv()
        gk = gk + gkr[k - 1].astype(F32)
    g_t[1] = gk.astype(BF)
    yk = half_start(1)
    low_t = low.astype(F32).T.astype(BF)
    lg = jnp.concatenate([mm_t(low_t, g_t[0]), mm_t(low_t, g_t[1])], axis=1)
    half_end(0, yq)
    half_end(1, yk)

    piece = pay.shape[0] // D
    part = piece // C
    kw = kbuf.shape[1]
    pr = proj[...]
    for b in range(kw // 256):
        out = mm(pr, kbuf[at(par * PC, PC, PC), b * 256 : (b + 1) * 256])
        pay[b * 256 : b * 256 + 128, :] = out[:, :128].astype(BF)
        pay[b * 256 + 128 : b * 256 + 256, :] = out[:, 128:].astype(BF)
    pay[kw : kw + rank, :] = lg.astype(BF)
    l0 = jnp.broadcast_to(loss, (16, 128))
    hi = l0.astype(BF)
    pay[kw + rank : kw + rank + 16, :] = hi
    pay[kw + rank + 16 : kw + rank + 32, :] = (l0 - hi.astype(F32)).astype(BF)
    pay[kw + rank + 32 :, :] = jnp.zeros((pay.shape[0] - kw - rank - 32, 128), BF)
    c1 = [
        send(pay.at[at(peer("dp", k) * piece, piece, 16)], r1.at[k - 1], "dp", peer("dp", k))
        for k in range(1, D)
    ]
    gdv = ADAPTER_SCALE * mm(adapter, pr)
    pw = PC // C
    for j in range(C):
        gd[j] = gdv[:, j * pw : (j + 1) * pw].astype(BF)
    cg = [(k, send(gd, gd_x.at[k // 2 - 1], "dp", peer("dp", k))) for k in range(2, D, 2)]

    lo = kw + rank

    def add_all(total, refs):
        for ref in refs:
            total = total + ref.astype(F32)
        return total

    for cp in c1:
        cp.wait_recv()
    p2[...] = add_all(
        pay[at(dp * piece, piece, 16), :].astype(F32), [r1[k] for k in range(D - 1)]
    ).astype(p2.dtype)
    c2 = [
        send(p2.at[at(peer("ctx", k) * part, part, 16)], r2.at[k - 1], "ctx", peer("ctx", k))
        for k in range(1, C)
    ]
    for _, cp in cg:
        cp.wait_recv()
    gd2[...] = add_all(gd[...].astype(F32), [gd_x[k // 2 - 1] for k, _ in cg]).astype(BF)
    cg2 = [
        send(gd2.at[peer("ctx", k)], gd_r.at[k - 1], "ctx", peer("ctx", k)) for k in range(1, C)
    ]
    for cp in c2:
        cp.wait_recv()
    r3[f] = add_all(
        p2[at(ctx * part, part, 16), :].astype(F32), [r2[k] for k in range(C - 1)]
    ).astype(r3.dtype)
    c3 = [send(r3.at[f], r3.at[f], "fsdp", peer("fsdp", k)) for k in range(1, F)]
    for cp in cg2:
        cp.wait_recv()
    gd_all[par, ctx] = add_all(gd2[ctx].astype(F32), [gd_r[k] for k in range(C - 1)]).astype(BF)
    cg3 = [
        send(gd_all.at[par, ctx], gd_all.at[par, ctx], "ctx", peer("ctx", k))
        for k in range(1, C)
    ]
    for cp in c3:
        cp.wait_recv()
    mine = at(dp * piece + ctx * part, part, 16)
    fin[mine, :] = add_all(jnp.zeros((part, 128), F32), [r3[k] for k in range(F)]).astype(fin.dtype)
    c4 = [send(fin.at[mine], fin.at[mine], "ctx", peer("ctx", k)) for k in range(1, C)]
    for cp in cg3:
        cp.wait_recv()
    cg4 = send(gd_all.at[par], gd_all.at[par], "dp", mate)
    for cp in c4:
        cp.wait_recv()
    mine = at(dp * piece, piece, 16)
    c5 = [send(fin.at[mine], fin.at[mine], "dp", peer("dp", k)) for k in range(1, D)]
    cg4.wait_recv()
    o_down[...] = gd_all[...].astype(F32)
    for cp in c5:
        cp.wait_recv()

    low_grad = fin[kw : kw + rank, :].astype(BF)
    o_up[...] = ADAPTER_SCALE * mm_t(low_grad, hd)
    lg_t = low_grad.astype(F32).T.astype(BF)
    for b in range(kw // 128):
        up_b = mm(lg_t, up[:, b * 128 : (b + 1) * 128])
        o_grad[b * 128 : (b + 1) * 128, :] = (
            fin[b * 128 : (b + 1) * 128, :].astype(F32) + ADAPTER_SCALE * up_b
        ).T
    o_loss[...] = (
        fin[lo : lo + 8, :].astype(F32) + fin[lo + 16 : lo + 24, :].astype(F32)
    ) * (1.0 / (seqs_all * count * C))
    for cp in sent:
        cp.wait_send()


def on_device(
    box_hidden_states,
    box_token_positions,
    document_lengths,
    successors,
    fixed_key_matrix,
    adapter_down,
    adapter_up,
    pointer_query_map,
    pointer_key_map,
):
    D, F, C = lax.axis_size("dp"), lax.axis_size("fsdp"), lax.axis_size("ctx")
    h = box_hidden_states[0]
    count, rows_all = h.shape
    RF = fixed_key_matrix.shape[0]
    PC = RF // 2
    kw = fixed_key_matrix.shape[1]
    width = pointer_query_map.shape[1]
    rank = adapter_up.shape[0]
    heads = jnp.concatenate([pointer_query_map, pointer_key_map], axis=1)
    unit = D * C * 16
    total = -(-(kw + rank + 32) // unit) * unit
    piece = total // D
    part = piece // C
    V = pltpu.VMEM
    n_sent = (
        2 * (F - 1) * 2 + 2 * (C - 1) + 2 * (F + F - 1) + (D - 1) + (D // 2 - 1)
        + 2 * (C - 1) + (F - 1) + 2 * (C - 1) + 1 + (D - 1)
    )
    vm = pl.BlockSpec(memory_space=pltpu.VMEM)
    hbm = pl.BlockSpec(memory_space=pl.ANY)
    grad, up_grad, down_g, loss = pl.pallas_call(
        functools.partial(kernel, D, F, C, D * F),
        out_shape=(
            jax.ShapeDtypeStruct((kw, 2 * width), F32),
            jax.ShapeDtypeStruct((rank, kw), F32),
            jax.ShapeDtypeStruct((2, C, rank, PC // C), F32),
            jax.ShapeDtypeStruct((8, 128), F32),
        ),
        in_specs=[hbm, hbm] + [vm] * 6,
        out_specs=(vm, vm, vm, vm),
        scratch_shapes=[
            V((count, rows_all), BF),
            V((RF, kw), BF),
            V((rows_all, 2 * width), BF),
            V((count, 2 * width), F32),
            V((count, rank), F32),
            V((count, 2 * width), BF),
            V((2 * width, count), BF),
            V((C, width, count), BF),
            V((count, C * count), BF),
            V((count, 128), F32),
            V((count, 128), F32),
            V((C - 1, width, count), BF),
            V((C - 1, width, count), BF),
            V((2, width, count), BF),
            V((2, F, width, PC), BF),
            V((2, F, width, PC), BF),
            V((2, F, width, PC), F32),
            V((2, F - 1, width, PC), BF),
            V((2, F - 1, width, PC), BF),
            V((2 * width, PC), BF),
            V((total, 128), BF),
            V((D - 1, piece, 128), BF),
            V((piece, 128), BF),
            V((C - 1, part, 128), BF),
            V((part, 128), BF),
            V((F, part, 128), BF),
            V((total, 128), BF),
            V((C, rank, PC // C), BF),
            V((max(D // 2 - 1, 1), C, rank, PC // C), BF),
            V((C, rank, PC // C), BF),
            V((C - 1, rank, PC // C), BF),
            V((2, C, rank, PC // C), BF),
            pltpu.SemaphoreType.DMA((4 + F,)),
            pltpu.SemaphoreType.DMA((n_sent,)),
            pltpu.SemaphoreType.DMA((n_sent,)),
        ],
        compiler_params=pltpu.CompilerParams(
            collective_id=0, has_side_effects=True, vmem_limit_bytes=56 * 1024 * 1024
        ),
    )(
        h, fixed_key_matrix, adapter_down.T, adapter_up, heads,
        box_token_positions, document_lengths, successors,
    )
    return (
        down_g.transpose(0, 1, 3, 2).reshape(RF, rank),
        up_grad,
        grad[:, :width],
        grad[:, width:],
        loss[0, 0],
    )


def solution(mesh):
    in_specs = (
        P(("dp", "fsdp"), "ctx", None),
        P(("dp", "fsdp"), None),
        P(("dp", "fsdp"), None),
        P(("dp", "fsdp"), "ctx"),
        P("fsdp", None),
        P(),
        P(),
        P(),
        P(),
    )
    out_specs = (P("fsdp", None), P(), P(), P(), P())
    return jax.shard_map(
        on_device, mesh=mesh, in_specs=in_specs, out_specs=out_specs, check_vma=False
    )
```

time: 446 us -> 83.6 us (0.19)
  waiting for transfers between devices: 321 us -> 0 us
  Pallas kernels: 0 us -> 71.5 us
  blocking collectives: 53.1 us -> 0 us
  matrix products: 47.9 us -> 0 us
  between operations: 15.7 us -> 0.66 us
  local copies, waits for them, and re-layouts: 1.7 us -> 9.99 us
  other arithmetic: 5.73 us -> 0.85 us
    all_gather x1 -> x0, waiting for transfers between devices: 197 us -> none  [on_device(): complete_keys = lax.all_gather(fixed_key_matrix, 'fsdp', axis=0, tiled=True)]
    psum x1 -> x0, waiting for transfers between devices: 102 us -> none  [on_device(): lax.psum((grad_down, projection_gradient, narrow_rows_gradient, loss_part...]
    pallas_call x0 -> x1, Pallas kernels: none -> 71.5 us  [on_device(): pl.pallas_call(functools.partial(kernel, D, F, C, D * F), out_shape=(jax....]
    dot_general x13 -> x0, matrix products: 47.9 us -> none  [the longest x4 13.7 us: contract_rows(): lax.dot_general(left, right, (((0,), (0,)), ((), ())), preferred_element_...]
    psum x1 -> x0, blocking collectives: 39.2 us -> none  [on_device(): lax.psum((grad_down, projection_gradient, narrow_rows_gradient, loss_part...]
    reduce_scatter x1 -> x0, waiting for transfers between devices: 21.2 us -> none  [on_device(): lax.psum_scatter(contract_rows(weights, queries), 'ctx', scatter_dimensio...]
    all_gather x1 -> x0, blocking collectives: 13.9 us -> none  [on_device(): all_keys = lax.all_gather(keys, 'ctx', axis=0, tiled=True)]
    unnamed x17 -> x5, local copies, waits for them, and re-layouts: 0.05 us -> 5.4 us
  transfers between devices with their start and end apart: 3 -> 0, of which waited for: 3 -> 0; matrix products, arithmetic and copies ran while one was open for 2% -> 0% of each run, Pallas kernels for 0% -> 0%
where the time goes in v1:
time: 83.6 us; the launch traced here: 83 us
  Pallas kernels  71.5 us (86%)
  local copies, waits for them, and re-layouts  9.99 us (12%)
  other arithmetic  0.85 us (1%)
    pallas_call x1, Pallas kernels, on_device(): pl.pallas_call(functools.partial(kernel, D, F, C, D * F), out_shape=(jax....  71.5 us
    unnamed x5, local copies, waits for them, and re-layouts  5.4 us

profile of v1, /device:TPU:0, one launch (start us, length us, event | category | flops | bytes accessed | tf_op | source)
XLA Modules:
  0.0 83.0 jit_solution(17766263658214144487)
XLA Ops:
  0.6 1.1 %copy.18 = bf16[1024,64]{1,0:T(8,128)(2,1)S(1)} copy(bf16[1024,64]{0,1:T(8,128)(2,1)} %param.16) | data formatting | bytes 262144 | tf_op args[7]
  1.7 1.1 %copy.19 = bf16[1024,64]{1,0:T(8,128)(2,1)S(1)} copy(bf16[1024,64]{0,1:T(8,128)(2,1)} %param.17) | data formatting | bytes 262144 | tf_op args[8]
  2.8 0.9 %pad_maximum_fusion.heads = bf16[1024,128]{1,0:T(8,128)(2,1)} fusion(bf16[1024,64]{1,0:T(8,128)(2,1)S(1)} %copy.19, bf16[1024,64]{1,0:T(8,128)(2,1)S(1)} %copy.18), kind=kLoop, calls=%fused_computation | loop fusion | flops 524288 | bytes 524288 | tf_op jit(solution)/shard_map/concatenate | solution.py:374
  3.6 71.5 %shard_map.128 = (f32[1024,128]{1,0:T(8,128)}, f32[16,1024]{1,0:T(8,128)}, f32[2,4,16,512]{3,2,1,0:T(8,128)}, f32[8,128]{1,0:T(8,128)}) custom-call(bf16[512,8192]{1,0:T(8,128)(2,1)} %bitcast.6, bf16[4096,1024]{1,0:T(8,128)(2,1)} %k_hbm.1, bf16[16,8192]{1,0:T(8,128)(2,1)} %bitcast.7, bf16[16,1024]{1,0:T(8,128)(2,1)} %up.1, ...), custom_call_target="tpu_custom_call" | custom-call | tf_op jit(solution)/shard_map/pallas_call | solution.py:386
  75.2 1.2 %slice.11 = f32[1,1]{1,0:T(1,128)} slice(f32[8,128]{1,0:T(8,128)} %get-tuple-element.12), slice={[0:1], [0:1]} | slice | bytes 8 | tf_op jit(solution)/shard_map/slice | solution.py:445
  76.4 1.1 %copy.20 = f32[2,4,512,16]{2,1,0,3:T(4,128)S(1)} copy(f32[2,4,512,16]{2,3,1,0:T(8,128)} %bitcast.8) | data formatting | bytes 524288 | tf_op jit(solution)/shard_map/transpose | solution.py:441
  77.5 0.9 %reshape.13 = f32[4096,16]{0,1:T(8,128)} reshape(f32[2,4,512,16]{2,1,0,3:T(4,128)S(1)} %copy.20) | data formatting | bytes 524288 | tf_op jit(solution)/shard_map/reshape | solution.py:441
  78.4 1.4 %fusion = (f32[1024,64]{1,0:T(8,128)S(1)}, f32[1024,64]{1,0:T(8,128)S(1)}) fusion(f32[1024,128]{1,0:T(8,128)} %get-tuple-element.11), kind=kLoop, calls=%fused_computation.1 | loop fusion | bytes 1048576 | tf_op jit(solution)/shard_map/slice | solution.py:444
  79.8 0.9 %copy.22 = f32[1024,64]{0,1:T(8,128)} copy(f32[1024,64]{1,0:T(8,128)S(1)} %get-tuple-element.23) | data formatting | bytes 524288
  80.7 0.9 %copy.21 = f32[1024,64]{0,1:T(8,128)} copy(f32[1024,64]{1,0:T(8,128)S(1)} %get-tuple-element.24) | data formatting | bytes 524288
  81.6 1.5 %copy.24 = f32[16,1024]{1,0:T(8,128)} copy(f32[16,1024]{1,0:T(8,128)} %get-tuple-element.31) | data formatting | bytes 131072

commit v2 on v1

v2 whole, which is shorter than its diff:
```python
import functools
import math

import jax
import jax.numpy as jnp
from jax import lax
from jax.experimental import pallas as pl
from jax.experimental.pallas import tpu as pltpu
from jax.sharding import PartitionSpec as P

ADAPTER_SCALE = 0.5
BF = jnp.bfloat16
F32 = jnp.float32


def mm(a, b):
    return lax.dot_general(a, b, (((1,), (0,)), ((), ())), preferred_element_type=F32)


def mm_t(a, b):
    return lax.dot_general(a, b, (((1,), (1,)), ((), ())), preferred_element_type=F32)


def at(start, size, unit):
    return pl.ds(pl.multiple_of(start, unit), size)


def kernel(
    D, F, C, seqs_all,
    h_hbm, k_hbm, down_t, up, qmap_t, kmap_t, pos, lengths, succ,
    fin, gd_all,
    hd, hbuf, kbuf, pbuf, acc, lowacc, bl, blt, keys_t, wts, seg_col, succ_col,
    gks, gkr, g_t, core_s, core_r, own, y_s, y_r, proj,
    pay, r1, p2, r2, r3, gd, gd_x, gd2, gd_r,
    load_sem, send_sem, recv_sem,
):
    rows_all, rank = hbuf.shape[1], up.shape[0]
    count, width = hbuf.shape[0], bl.shape[1] // 2
    RF = rows_all // F
    PC = RF // 2
    NS = min(4, PC // 256)
    SUB = PC // (2 * NS)
    dp, f, ctx = lax.axis_index("dp"), lax.axis_index("fsdp"), lax.axis_index("ctx")
    par = lax.rem(dp, 2)
    mate = dp + 1 - 2 * par
    other = 1 - par
    near = (dp // 2) * NS * SUB
    far = NS * SUB - near
    across = lax.rem(dp + D // 2, D)

    loads = []

    def load(src, dst):
        cp = pltpu.make_async_copy(src, dst, load_sem.at[len(loads)])
        cp.start()
        loads.append(cp)
        return cp

    def load_rows(start, n):
        r = at(start, n, SUB)
        return load(k_hbm.at[r], kbuf.at[r])

    lk = [load_rows(par * PC + near, NS * SUB), load_rows(par * PC + far, NS * SUB)]
    lk.append(load_rows(other * PC, PC))
    lh = []
    for k in range(F):
        cols = at(lax.rem(f + k, F) * RF, RF, 128)
        lh.append(load(h_hbm.at[:, cols], hbuf.at[:, cols]))

    axes = {"dp": (dp, D), "fsdp": (f, F), "ctx": (ctx, C)}

    def peer(axis, k):
        me, n = axes[axis]
        return lax.rem(me + k, n)

    barrier = pltpu.get_barrier_semaphore()
    for axis in axes:
        for k in range(1, axes[axis][1]):
            pl.semaphore_signal(
                barrier, inc=1, device_id={axis: peer(axis, k)},
                device_id_type=pl.DeviceIdType.MESH,
            )

    sent = []

    def send(src, dst, axis, target):
        i = len(sent)
        cp = pltpu.make_async_remote_copy(
            src_ref=src, dst_ref=dst, send_sem=send_sem.at[i], recv_sem=recv_sem.at[i],
            device_id={axis: target}, device_id_type=pl.DeviceIdType.MESH,
        )
        cp.start()
        sent.append(cp)
        return cp

    hd_t = jnp.concatenate([qmap_t[...], kmap_t[...]], axis=0)
    hd[...] = hd_t.astype(F32).T.astype(BF)

    def pointer_rows(start, n):
        tile = min(512, n)

        def body(t, _):
            r = start + t * tile
            pbuf[at(f * RF + r, tile, 64), :] = mm(kbuf[at(r, tile, 64), :], hd[...]).astype(BF)
            return 0
        lax.fori_loop(0, n // tile, body, 0)

    def grows(g, p, part_of, s):
        return at(g * RF + p * PC + part_of + s * SUB, SUB, SUB)

    ysend = {}
    lk[0].wait()
    pointer_rows(par * PC + near, NS * SUB)
    pl.semaphore_wait(barrier, (D - 1) + (F - 1) + (C - 1))
    for s in range(NS):
        for k in range(1, F):
            r = grows(f, par, near, s)
            ysend[s, k] = send(pbuf.at[r], pbuf.at[r], "fsdp", peer("fsdp", k))
    lk[1].wait()
    pointer_rows(par * PC + far, NS * SUB)
    lk[2].wait()
    pointer_rows(other * PC, PC)

    adapter = mm(up[...], hd[...]).astype(BF)

    def add_rows(start, n):
        tile = min(1024, n)

        def body(t, _):
            c = at(start + t * tile, tile, 128)
            acc[...] += mm(hbuf[:, c], pbuf[at(start + t * tile, tile, 128), :])
            return 0
        lax.fori_loop(0, n // tile, body, 0)

    acc[...] = jnp.zeros_like(acc)
    lowacc[...] = jnp.zeros_like(lowacc)
    for k in range(F):
        lh[k].wait()

    def to_column(row):
        return jnp.broadcast_to(row, (128, count)).T

    def segment_of(p):
        end = jnp.zeros((1, 1), jnp.int32)
        total = jnp.zeros(p.shape, F32)
        for n in range(lengths.shape[1] - 1):
            end = end + lengths[:, n : n + 1]
            total = total + jnp.where(p >= end, 1.0, 0.0)
        return total

    seg_row = segment_of(pos[...])
    seg_col[...] = to_column(segment_of(pos[:, at(ctx * count, count, 128)]))
    succ_col[...] = to_column(succ[...].astype(F32))

    low_tile = rows_all // NS
    xsend, relay_y, relay_x = {}, {}, {}

    def take_x(s):
        for k in range(1, F):
            g = peer("fsdp", F - k)
            xsend[s, k].wait_recv()
            r = grows(g, par, far, s)
            relay_x[s, k] = send(pbuf.at[r], pbuf.at[r], "dp", mate)

    for s in range(NS):
        for k in range(1, F):
            g = peer("fsdp", F - k)
            ysend[s, k].wait_recv()
            r = grows(g, par, near, s)
            xsend[s, k] = send(pbuf.at[r], pbuf.at[r], "dp", across)
            relay_y[s, k] = send(pbuf.at[r], pbuf.at[r], "dp", mate)
        add_rows(f * RF + s * (RF // NS), RF // NS)
        if s:
            take_x(s - 1)
        c = slice(s * low_tile, (s + 1) * low_tile)
        lowacc[...] += mm_t(hbuf[:, c], down_t[:, c])
    low = lowacc[...].astype(BF)
    acc[...] += ADAPTER_SCALE * mm(low, adapter)
    take_x(NS - 1)
    for k in range(1, F):
        base = peer("fsdp", F - k) * RF
        add_rows(base + par * PC, PC)
        for s in range(NS):
            relay_y[s, k].wait_recv()
        add_rows(base + other * PC + near, NS * SUB)
        for s in range(NS):
            relay_x[s, k].wait_recv()
        add_rows(base + other * PC + far, NS * SUB)

    rounded = acc[...].astype(BF)
    bl[...] = rounded
    blt[...] = rounded.astype(F32).T.astype(BF)
    keys_t[ctx] = blt[width:, :]
    kcp = [
        send(keys_t.at[ctx], keys_t.at[ctx], "ctx", peer("ctx", k)) for k in range(1, C)
    ]
    for cp in kcp:
        cp.wait_recv()

    scale = 1.0 / math.sqrt(width)
    block = 64
    column = lax.broadcasted_iota(jnp.int32, (1, C * count), 1).astype(F32)

    def soft(t, loss):
        r = at(t * block, block, block)
        q = bl[r, :width]
        sc = jnp.concatenate([mm(q, keys_t[j]) for j in range(C)], axis=1) * scale
        masked = jnp.where(seg_col[r, 0:1] == seg_row, sc, -jnp.inf)
        top = jnp.max(masked, axis=1, keepdims=True)
        e = jnp.exp(masked - top)
        total = jnp.sum(e, axis=1, keepdims=True)
        hit = succ_col[r, 0:1] == column
        picked = jnp.sum(jnp.where(hit, sc, 0.0), axis=1, keepdims=True)
        ws = scale / seqs_all
        wts[r, :] = (e * (ws / total) - jnp.where(hit, ws, 0.0)).astype(BF)
        return loss + (top + jnp.log(total) - picked)

    loss = lax.fori_loop(0, count // block, soft, jnp.zeros((block, 1), F32))
    loss = jnp.sum(loss, axis=0, keepdims=True)

    q_t = blt[:width, :]
    gcp = []
    for k in range(1, C):
        c = at(peer("ctx", k) * count, count, 128)
        gks[k - 1] = mm(q_t, wts[:, c]).astype(BF)
        gcp.append(send(gks.at[k - 1], gkr.at[k - 1], "ctx", peer("ctx", k)))
    gq = mm_t(keys_t[0], wts[:, :count])
    for j in range(1, C):
        gq = gq + mm_t(keys_t[j], wts[:, j * count : (j + 1) * count])
    g_t[0] = gq.astype(BF)
    gk = mm(q_t, wts[:, at(ctx * count, count, 128)])

    ct = min(512, PC)

    def half_start(h):
        g = g_t[h]
        cps = []
        for k in list(range(1, F)) + [0]:
            base = peer("fsdp", k) * RF
            for t in range(PC // ct):
                core_s[h, k, :, t * ct : (t + 1) * ct] = mm(
                    g, hbuf[:, at(base + other * PC + t * ct, ct, 128)]
                ).astype(BF)
            cps.append((k, send(core_s.at[h, k], core_r.at[h, k], "dp", mate)))
        for k in range(F):
            base = peer("fsdp", k) * RF
            for t in range(PC // ct):
                own[h, k, :, t * ct : (t + 1) * ct] = mm(
                    g, hbuf[:, at(base + par * PC + t * ct, ct, 128)]
                )
        ys = []
        for k, cp in cps:
            cp.wait_recv()
            summed = own[h, k] + core_r[h, k].astype(F32)
            if k:
                y_s[h, k - 1] = summed.astype(BF)
                ys.append(
                    (k, send(y_s.at[h, k - 1], y_r.at[h, k - 1], "fsdp", peer("fsdp", k)))
                )
            else:
                own[h, 0] = summed
        return ys

    def half_end(h, ys):
        total = own[h, 0]
        for k, cp in ys:
            cp.wait_recv()
            total = total + y_r[h, k - 1].astype(F32)
        proj[h] = total.astype(BF)

    yq = half_start(0)
    for k in range(1, C):
        gcp[k - 1].wait_recv()
        gk = gk + gkr[k - 1].astype(F32)
    g_t[1] = gk.astype(BF)
    yk = half_start(1)
    low_t = low.astype(F32).T.astype(BF)
    lg = jnp.concatenate([mm_t(low_t, g_t[0]), mm_t(low_t, g_t[1])], axis=1)
    def add_all(total, refs):
        for ref in refs:
            total = total + ref.astype(F32)
        return total

    kw = kbuf.shape[1]
    body_rows = kw // 128 * width
    offset = (0, body_rows)
    sizes = (body_rows, pay.shape[0] - body_rows)

    def share(h):
        base = offset[h]
        pr = proj[h]
        for b in range(kw // 256):
            out = mm(pr, kbuf[at(par * PC, PC, 128), b * 256 : (b + 1) * 256])
            for u in (0, 1):
                r = base + (2 * b + u) * width
                pay[r : r + width, :] = out[:, u * 128 : (u + 1) * 128].astype(BF)
        if h:
            r = base + body_rows
            pay[r : r + rank, :] = lg.astype(BF)
            l0 = jnp.broadcast_to(loss, (16, 128))
            hi = l0.astype(BF)
            pay[r + rank : r + rank + 16, :] = hi
            pay[r + rank + 16 : r + rank + 32, :] = (l0 - hi.astype(F32)).astype(BF)
            r = r + rank + 32
            pay[r:, :] = jnp.zeros((pay.shape[0] - r, 128), BF)
        n = sizes[h] // D
        return [
            send(
                pay.at[at(base + peer("dp", k) * n, n, 16)], r1.at[h, k - 1, 0:n],
                "dp", peer("dp", k),
            )
            for k in range(1, D)
        ]

    def wait_all(cps):
        for cp in cps:
            cp.wait_recv()

    def over_ctx(h, cps):
        n = sizes[h] // D
        m = n // C
        wait_all(cps)
        p2[h, 0:n] = add_all(
            pay[at(offset[h] + dp * n, n, 16), :].astype(F32),
            [r1[h, k, 0:n] for k in range(D - 1)],
        ).astype(BF)
        return [
            send(
                p2.at[h, at(peer("ctx", k) * m, m, 16)], r2.at[h, k - 1, 0:m],
                "ctx", peer("ctx", k),
            )
            for k in range(1, C)
        ]

    def over_fsdp(h, cps):
        m = sizes[h] // D // C
        wait_all(cps)
        r3[h, f, 0:m] = add_all(
            p2[h, at(ctx * m, m, 16), :].astype(F32), [r2[h, k, 0:m] for k in range(C - 1)]
        ).astype(BF)
        mine = r3.at[h, f, 0:m]
        return [send(mine, mine, "fsdp", peer("fsdp", k)) for k in range(1, F)]

    def back_ctx(h, cps):
        n = sizes[h] // D
        m = n // C
        wait_all(cps)
        mine = at(offset[h] + dp * n + ctx * m, m, 16)
        fin[mine, :] = add_all(
            jnp.zeros((m, 128), F32), [r3[h, k, 0:m] for k in range(F)]
        ).astype(BF)
        return [send(fin.at[mine], fin.at[mine], "ctx", peer("ctx", k)) for k in range(1, C)]

    def back_dp(h, cps):
        n = sizes[h] // D
        wait_all(cps)
        mine = at(offset[h] + dp * n, n, 16)
        return [send(fin.at[mine], fin.at[mine], "dp", peer("dp", k)) for k in range(1, D)]

    half_end(0, yq)
    a0 = over_ctx(0, share(0))
    half_end(1, yk)
    a1 = share(1)
    gdv = ADAPTER_SCALE * (mm(adapter[:, :width], proj[0]) + mm(adapter[:, width:], proj[1]))
    pw = PC // C
    for j in range(C):
        gd[j] = gdv[:, j * pw : (j + 1) * pw].astype(BF)
    cg = [(k, send(gd, gd_x.at[k // 2 - 1], "dp", peer("dp", k))) for k in range(2, D, 2)]
    a0 = over_fsdp(0, a0)
    a1 = over_ctx(1, a1)
    a0 = back_ctx(0, a0)
    wait_all([cp for _, cp in cg])
    gd2[...] = add_all(gd[...].astype(F32), [gd_x[k // 2 - 1] for k, _ in cg]).astype(BF)
    cg2 = [
        send(gd2.at[peer("ctx", k)], gd_r.at[k - 1], "ctx", peer("ctx", k)) for k in range(1, C)
    ]
    a1 = over_fsdp(1, a1)
    a0 = back_dp(0, a0)
    wait_all(cg2)
    gd_all[par, ctx] = add_all(gd2[ctx].astype(F32), [gd_r[k] for k in range(C - 1)]).astype(BF)
    cg3 = [
        send(gd_all.at[par, ctx], gd_all.at[par, ctx], "ctx", peer("ctx", k))
        for k in range(1, C)
    ]
    a1 = back_ctx(1, a1)
    wait_all(cg3)
    cg4 = send(gd_all.at[par], gd_all.at[par], "dp", mate)
    a1 = back_dp(1, a1)
    wait_all(a0)
    wait_all(a1)
    cg4.wait_recv()
    for cp in sent:
        cp.wait_send()


def outputs(scale, fin, gd_all, up, qmap_t, kmap_t, o_q, o_k, o_up, o_down, o_loss):
    rank, kw = up.shape
    width = o_q.shape[0]
    body_rows = kw // 128 * width
    r = 2 * body_rows
    low_grad = fin[r : r + rank, :]
    hd_t = jnp.concatenate([qmap_t[...], kmap_t[...]], axis=0)
    o_up[...] = ADAPTER_SCALE * mm(low_grad, hd_t)
    lg_t = low_grad.astype(F32).T.astype(BF)
    upper = ADAPTER_SCALE * mm(lg_t, up[...])
    for h, o in ((0, o_q), (1, o_k)):
        for b in range(kw // 128):
            r0 = h * body_rows + b * width
            c = slice(b * 128, (b + 1) * 128)
            o[:, c] = fin[r0 : r0 + width, :].astype(F32) + upper[h * width : (h + 1) * width, c]
    halves, C, _, pw = gd_all.shape
    for p in range(halves):
        for j in range(C):
            at0 = (p * C + j) * pw
            o_down[:, at0 : at0 + pw] = gd_all[p, j].astype(F32)
    l0 = r + rank
    both = fin[l0 : l0 + 16, :].astype(F32) + fin[l0 + 16 : l0 + 32, :].astype(F32)
    o_loss[...] = both[0:1, 0:1] * scale


def on_device(
    box_hidden_states,
    box_token_positions,
    document_lengths,
    successors,
    fixed_key_matrix,
    adapter_down,
    adapter_up,
    pointer_query_map,
    pointer_key_map,
):
    D, F, C = lax.axis_size("dp"), lax.axis_size("fsdp"), lax.axis_size("ctx")
    h = box_hidden_states[0]
    count, rows_all = h.shape
    RF = fixed_key_matrix.shape[0]
    PC = RF // 2
    kw = fixed_key_matrix.shape[1]
    width = pointer_query_map.shape[1]
    rank = adapter_up.shape[0]
    unit = D * C * 16
    first = kw // 128 * width
    second = -(-(first + rank + 32) // unit) * unit
    total = first + second
    piece = second // D
    part = piece // C
    NS = min(4, PC // 256)
    V = pltpu.VMEM
    n_sent = (
        4 * NS * (F - 1) + 2 * (C - 1) + 2 * (F + F - 1) + (D // 2 - 1) + 2 * (C - 1) + 1
        + 2 * (2 * (D - 1) + 2 * (C - 1) + (F - 1))
    )
    vm = pl.BlockSpec(memory_space=pltpu.VMEM)
    hbm = pl.BlockSpec(memory_space=pl.ANY)
    qmap_t, kmap_t = pointer_query_map.T, pointer_key_map.T
    fin, gd_all = pl.pallas_call(
        functools.partial(kernel, D, F, C, D * F),
        out_shape=(
            jax.ShapeDtypeStruct((total, 128), BF),
            jax.ShapeDtypeStruct((2, C, rank, PC // C), BF),
        ),
        in_specs=[hbm, hbm] + [vm] * 7,
        out_specs=(vm, vm),
        scratch_shapes=[
            V((kw, 2 * width), BF),
            V((count, rows_all), BF),
            V((RF, kw), BF),
            V((rows_all, 2 * width), BF),
            V((count, 2 * width), F32),
            V((count, rank), F32),
            V((count, 2 * width), BF),
            V((2 * width, count), BF),
            V((C, width, count), BF),
            V((count, C * count), BF),
            V((count, 128), F32),
            V((count, 128), F32),
            V((C - 1, width, count), BF),
            V((C - 1, width, count), BF),
            V((2, width, count), BF),
            V((2, F, width, PC), BF),
            V((2, F, width, PC), BF),
            V((2, F, width, PC), F32),
            V((2, F - 1, width, PC), BF),
            V((2, F - 1, width, PC), BF),
            V((2, width, PC), BF),
            V((total, 128), BF),
            V((2, D - 1, piece, 128), BF),
            V((2, piece, 128), BF),
            V((2, C - 1, part, 128), BF),
            V((2, F, part, 128), BF),
            V((C, rank, PC // C), BF),
            V((max(D // 2 - 1, 1), C, rank, PC // C), BF),
            V((C, rank, PC // C), BF),
            V((C - 1, rank, PC // C), BF),
            pltpu.SemaphoreType.DMA((3 + F,)),
            pltpu.SemaphoreType.DMA((n_sent,)),
            pltpu.SemaphoreType.DMA((n_sent,)),
        ],
        compiler_params=pltpu.CompilerParams(
            collective_id=0, has_side_effects=True, vmem_limit_bytes=56 * 1024 * 1024
        ),
    )(
        h, fixed_key_matrix, adapter_down.T, adapter_up, qmap_t, kmap_t,
        box_token_positions, document_lengths, successors,
    )
    grad_q, grad_k, up_grad, down_t, loss = pl.pallas_call(
        functools.partial(outputs, 1.0 / (D * F * count * C)),
        out_shape=(
            jax.ShapeDtypeStruct((width, kw), F32),
            jax.ShapeDtypeStruct((width, kw), F32),
            jax.ShapeDtypeStruct((rank, kw), F32),
            jax.ShapeDtypeStruct((rank, RF), F32),
            jax.ShapeDtypeStruct((1, 1), F32),
        ),
        in_specs=[vm] * 5,
        out_specs=(vm,) * 5,
    )(fin, gd_all, adapter_up, qmap_t, kmap_t)
    return down_t.T, up_grad, grad_q.T, grad_k.T, loss[0, 0]


def solution(mesh):
    in_specs = (
        P(("dp", "fsdp"), "ctx", None),
        P(("dp", "fsdp"), None),
        P(("dp", "fsdp"), None),
        P(("dp", "fsdp"), "ctx"),
        P("fsdp", None),
        P(),
        P(),
        P(),
        P(),
    )
    out_specs = (P("fsdp", None), P(), P(), P(), P())
    return jax.shard_map(
        on_device, mesh=mesh, in_specs=in_specs, out_specs=out_specs, check_vma=False
    )
```

time: 83.6 us -> 72.7 us (0.87)
  local copies, waits for them, and re-layouts: 9.99 us -> 0 us
  other arithmetic: 0.85 us -> 0 us
    unnamed x5 -> x0, local copies, waits for them, and re-layouts: 5.4 us -> none
    slice x2 -> x0, local copies, waits for them, and re-layouts: 2.59 us -> none  [the longest x1 1.4 us: on_device(): grad[:, width:]]
    pallas_call x0 -> x1, Pallas kernels: none -> 2.27 us  [on_device(): pl.pallas_call(functools.partial(outputs, 1.0 / (D * F * count * C)), out...]
    pallas_call x1, Pallas kernels: 71.5 us -> 69.7 us  [on_device(): pl.pallas_call(functools.partial(kernel, D, F, C, D * F), out_shape=(jax....]
    transpose x1 -> x0, local copies, waits for them, and re-layouts: 1.12 us -> none  [on_device(): down_g.transpose(0, 1, 3, 2).reshape(RF, rank)]
    reshape x1 -> x0, local copies, waits for them, and re-layouts: 0.88 us -> none  [on_device(): down_g.transpose(0, 1, 3, 2).reshape(RF, rank)]
    concatenate x1 -> x0, other arithmetic: 0.85 us -> none  [on_device(): heads = jnp.concatenate([pointer_query_map, pointer_key_map], axis=1)]
where the time goes in v2:
time: 72.7 us; the launch traced here: 72.6 us
  Pallas kernels  71.9 us (99%)
    pallas_call x1, Pallas kernels, on_device(): pl.pallas_call(functools.partial(kernel, D, F, C, D * F), out_shape=(jax....  69.7 us
    pallas_call x1, Pallas kernels, on_device(): pl.pallas_call(functools.partial(outputs, 1.0 / (D * F * count * C)), out...  2.27 us

profile of v2, /device:TPU:0, one launch (start us, length us, event | category | flops | bytes accessed | tf_op | source)
XLA Modules:
  0.0 72.6 jit_solution(9238291205952622841)
XLA Ops:
  0.6 69.7 %shard_map.128 = (bf16[1280,128]{1,0:T(8,128)(2,1)}, bf16[2,4,16,512]{3,2,1,0:T(8,128)(2,1)}) custom-call(bf16[512,8192]{1,0:T(8,128)(2,1)} %bitcast.8, bf16[4096,1024]{1,0:T(8,128)(2,1)} %k_hbm.1, bf16[16,8192]{1,0:T(8,128)(2,1)} %bitcast.13, bf16[16,1024]{1,0:T(8,128)(2,1)} %up.3, bf16[64,1024]{1,0:T(8,128)(2,1)} %bitcast.9, bf16[64,1024]{1,0:T(8,128)(2,1)} %bitcast.11, ...), custom_call_target="tpu_custom_call" | custom-call | tf_op jit(solution)/shard_map/pallas_call | solution.py:455
  70.3 2.3 %shard_map.129 = (f32[64,1024]{1,0:T(8,128)}, f32[64,1024]{1,0:T(8,128)}, f32[16,1024]{1,0:T(8,128)}, f32[16,4096]{1,0:T(8,128)}, f32[1,1]{1,0:T(1,128)}) custom-call(bf16[1280,128]{1,0:T(8,128)(2,1)} %get-tuple-element.12.fin, bf16[2,4,16,512]{3,2,1,0:T(8,128)(2,1)} %get-tuple-element.13.gd_all, bf16[16,1024]{1,0:T(8,128)(2,1)} %up.3, ...), custom_call_target="tpu_custom_call" | custom-call | tf_op jit(solution)/shard_map/pallas_call | solution.py:505

commit v3 on v2

--- a/solution.py
+++ b/solution.py
@@ -108,6 +108,25 @@
     def grows(g, p, part_of, s):
         return at(g * RF + p * PC + part_of + s * SUB, SUB, SUB)
 
+    adapter = mm(up[...], hd[...]).astype(BF)
+
+    acc[...] = jnp.zeros_like(acc)
+    lowacc[...] = jnp.zeros_like(lowacc)
+    def to_column(row):
+        return jnp.broadcast_to(row, (128, count)).T
+
+    def segment_of(p):
+        end = jnp.zeros((1, 1), jnp.int32)
+        total = jnp.zeros(p.shape, F32)
+        for n in range(lengths.shape[1] - 1):
+            end = end + lengths[:, n : n + 1]
+            total = total + jnp.where(p >= end, 1.0, 0.0)
+        return total
+
+    seg_row = segment_of(pos[...])
+    seg_col[...] = to_column(segment_of(pos[:, at(ctx * count, count, 128)]))
+    succ_col[...] = to_column(succ[...].astype(F32))
+
     ysend = {}
     lk[0].wait()
     pointer_rows(par * PC + near, NS * SUB)
@@ -121,8 +140,6 @@
     lk[2].wait()
     pointer_rows(other * PC, PC)
 
-    adapter = mm(up[...], hd[...]).astype(BF)
-
     def add_rows(start, n):
         tile = min(1024, n)
 
@@ -132,25 +149,8 @@
             return 0
         lax.fori_loop(0, n // tile, body, 0)
 
-    acc[...] = jnp.zeros_like(acc)
-    lowacc[...] = jnp.zeros_like(lowacc)
     for k in range(F):
         lh[k].wait()
-
-    def to_column(row):
-        return jnp.broadcast_to(row, (128, count)).T
-
-    def segment_of(p):
-        end = jnp.zeros((1, 1), jnp.int32)
-        total = jnp.zeros(p.shape, F32)
-        for n in range(lengths.shape[1] - 1):
-            end = end + lengths[:, n : n + 1]
-            total = total + jnp.where(p >= end, 1.0, 0.0)
-        return total
-
-    seg_row = segment_of(pos[...])
-    seg_col[...] = to_column(segment_of(pos[:, at(ctx * count, count, 128)]))
-    succ_col[...] = to_column(succ[...].astype(F32))
 
     low_tile = rows_all // NS
     xsend, relay_y, relay_x = {}, {}, {}

time: 72.7 us -> 72.6 us (level)
  no operation moved by 1% of the time
where the time goes in v3:
time: 72.6 us; the launch traced here: 72.5 us
  Pallas kernels  71.8 us (99%)
    pallas_call x1, Pallas kernels, on_device(): pl.pallas_call(functools.partial(kernel, D, F, C, D * F), out_shape=(jax....  69.5 us
    pallas_call x1, Pallas kernels, on_device(): pl.pallas_call(functools.partial(outputs, 1.0 / (D * F * count * C)), out...  2.27 us

profile of v3, /device:TPU:0, one launch (start us, length us, event | category | flops | bytes accessed | tf_op | source)
XLA Modules:
  0.0 72.5 jit_solution(5173319394228181655)
XLA Ops:
  0.6 69.5 %shard_map.128 = (bf16[1280,128]{1,0:T(8,128)(2,1)}, bf16[2,4,16,512]{3,2,1,0:T(8,128)(2,1)}) custom-call(bf16[512,8192]{1,0:T(8,128)(2,1)} %bitcast.8, bf16[4096,1024]{1,0:T(8,128)(2,1)} %k_hbm.1, bf16[16,8192]{1,0:T(8,128)(2,1)} %bitcast.13, bf16[16,1024]{1,0:T(8,128)(2,1)} %up.3, bf16[64,1024]{1,0:T(8,128)(2,1)} %bitcast.9, bf16[64,1024]{1,0:T(8,128)(2,1)} %bitcast.11, ...), custom_call_target="tpu_custom_call" | custom-call | tf_op jit(solution)/shard_map/pallas_call | solution.py:455
  70.2 2.3 %shard_map.129 = (f32[64,1024]{1,0:T(8,128)}, f32[64,1024]{1,0:T(8,128)}, f32[16,1024]{1,0:T(8,128)}, f32[16,4096]{1,0:T(8,128)}, f32[1,1]{1,0:T(1,128)}) custom-call(bf16[1280,128]{1,0:T(8,128)(2,1)} %get-tuple-element.12.fin, bf16[2,4,16,512]{3,2,1,0:T(8,128)(2,1)} %get-tuple-element.13.gd_all, bf16[16,1024]{1,0:T(8,128)(2,1)} %up.3, ...), custom_call_target="tpu_custom_call" | custom-call | tf_op jit(solution)/shard_map/pallas_call | solution.py:505
